TPU v7x, 32 devices: a whole 2x2x4 slice. The times are simulated.
32 devices in a mesh: user: 4 (over z), item: 8 (over y, x, core).
Axes of the slice: x: 2, y: 2, z: 4, core: 2. Of those that a mesh axis runs over, the one named last changes fastest.
Arguments:
- values: bfloat16 [4, 8, 256, 128], P('user', 'item'), may hold values from -6 to 6
- block_user: int32 [4, 8, 256], P('user', 'item'), may hold values from 0 to 63
- block_item: int32 [4, 8, 256], P('user', 'item'), may hold values from 0 to 2047
- block_ctx: int32 [4, 8, 256], P('user', 'item'), may hold values from 0 to 128
- block_count: int32 [4, 8], P('user', 'item'), may hold values from 64 to 256, as said below
- core: bfloat16 [32, 32, 32], replicated, may hold values from -1 to 1
- item_factor: bfloat16 [16384, 32], P(('item', 'user')), may hold values from -6 to 6
- ctx_factor: bfloat16 [256, 32], replicated, may hold values from -0.03125 to 0.03125
Outputs:
- user_factor: float32 [256, 32], P('user')
Inputs may be any that keep to these rules, and one draw needn't show every extreme that they name: A tile's live slots are its first block_count slots; some tile has all 256 slots live in every draw.
All inputs are finite; a program needn't handle non-finite values.
Results may differ from a plain program's by a relative error of at most 0.0047.
Values may be sent and summed in bfloat16 or wider, within the bound.
A program may use at most 64 MiB of HBM per device.

v0:
```python
import functools

import jax
import jax.numpy as jnp
from jax import lax
from jax.experimental import pallas as pl
from jax.experimental.pallas import tpu as pltpu
from jax.sharding import PartitionSpec as P

U_SH = 64
RIDGE = 0.1
MESH = pl.DeviceIdType.MESH
F32 = jnp.float32
BF16 = jnp.bfloat16
NT = (((1,), (1,)), ((), ()))


def iota(shape, dim):
    return lax.broadcasted_iota(jnp.int32, shape, dim)


def lanes_of(x, index):
    return jnp.take_along_axis(x, index, axis=1, mode="promise_in_bounds")


def solve(mats, target):
    shape = mats[0].shape
    lane = iota(shape, 1)
    block, place = lane >> 5, lane & 31
    count = len(mats)
    mats = [m + jnp.where(place == 4 * j + block, RIDGE, 0.0) for j, m in enumerate(mats)]
    cols = [lanes_of(target, 4 * j + block) for j in range(count)]
    for k in range(4 * count):
        jk, ck = divmod(k, 4)
        pivot = lanes_of(mats[jk], jnp.full(shape, ck * 32 + k, jnp.int32))
        row = lanes_of(mats[jk], ck * 32 + place)
        rhs = lanes_of(cols[jk], ck * 32 + place)
        factor = [lanes_of(m, (block << 5) + k) for m in mats]
        factor[jk] = jnp.where(block == ck, 0.0, factor[jk])
        inverse = 1.0 / pivot
        row, rhs = row * inverse, rhs * inverse
        mats = [m - f * row for m, f in zip(mats, factor)]
        cols = [c - f * rhs for c, f in zip(cols, factor)]
    answer = jnp.zeros(shape, F32)
    for j in range(count):
        x = cols[j] / lanes_of(mats[j], (block << 5) + 4 * j + block)
        answer = jnp.where((lane >> 2) == j, lanes_of(x, (lane & 3) << 5), answer)
    return answer


def kernel(
    n_user, n_item,
    values, b_user, b_item, b_ctx, b_count, core, item, ctx, out,
    fac, starts, bt, yb, rf, gb, pay, recv, xg,
    fac_send, fac_recv, pay_send, pay_recv, x_send, x_recv,
):
    me_u, me_i = lax.axis_index("user"), lax.axis_index("item")
    slots, bw = values.shape[2], values.shape[3]
    rank = core.shape[0]
    rows = item.shape[0]
    quarter = rows // 4
    packs = rank // 4
    per = U_SH // n_item

    barrier = pltpu.get_barrier_semaphore()
    for d in range(1, n_user):
        pl.semaphore_signal(barrier, inc=1, device_id={"user": lax.rem(me_u + d, n_user)}, device_id_type=MESH)
    for d in range(1, n_item):
        pl.semaphore_signal(barrier, inc=1, device_id={"item": lax.rem(me_i + d, n_item)}, device_id_type=MESH)

    own = item[...].astype(F32)
    fac[0] = jnp.concatenate([own[c * quarter : (c + 1) * quarter] for c in range(4)], axis=1).astype(BF16)
    pl.semaphore_wait(barrier, n_user + n_item - 2)
    fac_copies = []
    for d in range(1, n_user):
        copy = pltpu.make_async_remote_copy(
            src_ref=fac.at[0], dst_ref=fac.at[d], send_sem=fac_send.at[d], recv_sem=fac_recv.at[d],
            device_id={"user": lax.rem(me_u + d, n_user)}, device_id_type=MESH,
        )
        copy.start()
        fac_copies.append(copy)

    ids = b_item[0]
    starts_row = b_ctx[0]
    parts = [jnp.broadcast_to(r.astype(F32), (128, slots)) for r in (starts_row, ids >> 7, ids & 127)]
    eye = (iota((slots, slots), 0) == iota((slots, slots), 1)).astype(F32).astype(BF16)
    columns = lax.dot_general(eye, jnp.concatenate(parts, axis=0).astype(BF16), NT, preferred_element_type=F32)
    start_col = columns[:, :128].astype(jnp.int32)
    item_col = (columns[:, 128:256] * 128.0 + columns[:, 256:384]).astype(jnp.int32)
    starts[...] = start_col

    turned = values[0, 0].astype(F32)
    for bit in range(bw.bit_length() - 1):
        turned = jnp.where(((start_col >> bit) & 1) == 1, pltpu.roll(turned, 1 << bit, 1), turned)
    rf[pl.ds(rank * slots, slots), :] = turned
    rf[pl.ds((rank + 1) * slots, slots), :] = jnp.zeros((slots, bw), F32)

    cores = core[...].astype(F32)
    mixing = jnp.concatenate([cores[a] for a in range(rank)], axis=1)
    mixing = jnp.concatenate([mixing] * 4, axis=0).astype(BF16)
    ctx_rows = jnp.concatenate([ctx[...].astype(F32)] * 4, axis=1)
    ctx_block = iota(ctx_rows.shape, 1) >> 5
    for c in range(4):
        bt[c] = jnp.where(ctx_block == c, ctx_rows, 0.0).astype(BF16)
    live = iota((U_SH, slots), 1) < b_count[...]
    onehot = jnp.where((iota((U_SH, slots), 0) == b_user[0]) & live, 1.0, 0.0).astype(BF16)

    wide = n_user * quarter
    lane = iota((slots, wide), 1)
    owner = (me_u - (lane >> (quarter.bit_length() - 1)) + n_user) & (n_user - 1)
    held = owner * rows + (lane & (quarter - 1))
    wanted = jnp.concatenate([item_col] * (wide // 128), axis=1)
    picks = [jnp.where(held + c * quarter == wanted, 1.0, 0.0).astype(BF16) for c in range(4)]

    for copy in fac_copies:
        copy.wait()
    table = fac[...].reshape(wide, 128)
    slot_block = iota((slots, 128), 1) >> 5
    chosen = jnp.zeros((slots, 128), F32)
    for c in range(4):
        got = jnp.dot(picks[c], table, preferred_element_type=F32)
        chosen = jnp.where(slot_block == c, got, chosen)
    proj = jnp.dot(chosen.astype(BF16), mixing, preferred_element_type=F32).astype(BF16)
    for j in range(packs):
        yb[j] = proj[:, 128 * j : 128 * (j + 1)]

    def features(j, carry):
        first = iota((slots, bw), 1) >= starts[...]
        z = yb[j]
        for c in range(4):
            full = lax.dot_general(z, bt[c], NT, preferred_element_type=F32)
            rf[pl.ds(pl.multiple_of((4 * j + c) * slots, slots), slots), :] = jnp.where(first, full[:, :bw], full[:, bw:])
        return carry

    lax.fori_loop(0, packs, features, 0)

    def grams(g, carry):
        base = pl.multiple_of(8 * g, 8)
        left = jnp.concatenate([rf[pl.ds(a * slots + base, 8), :] for a in range(rank + 2)], axis=0).astype(BF16)
        right = jnp.concatenate([rf[pl.ds(base + s, rank, stride=slots), :] for s in range(8)], axis=0).astype(BF16)
        full = lax.dot_general(left, right, NT, preferred_element_type=F32)
        sub, ln = iota((8, 128), 0), iota((8, 128), 1)
        low, same = sub < 4, (ln >> 5) == (sub & 3)
        for a in range(rank + 1):
            part = full[8 * a : 8 * a + 8]
            gb[pl.ds(a * slots + base, 8), :] = jnp.where(same, jnp.where(low, part[:, :128], part[:, 128:]), 0.0)
        return carry

    lax.fori_loop(0, slots // 8, grams, 0)

    def summed(a):
        x = gb[pl.ds(pl.multiple_of(a * slots, slots), slots), :]
        high = x.astype(BF16)
        rest = (x - high.astype(F32)).astype(BF16)
        both = jnp.dot(onehot, jnp.concatenate([high, rest], axis=1), preferred_element_type=F32)
        return both[:, :128] + both[:, 128:]

    if per < 8:
        pay[...] = jnp.zeros(pay.shape, F32)

    def put(j, x):
        for q in range(n_item):
            pay[q, j, 0:per, :] = x[q * per : (q + 1) * per]

    def segments(j, carry):
        blk = iota((U_SH, 128), 1) >> 5
        x, w, y, v = (summed(4 * j + c) for c in range(4))
        low, mid, even = blk < 2, (blk == 1) | (blk == 2), (blk & 1) == 0
        one = jnp.where(low, x, y) + pltpu.roll(jnp.where(low, y, x), 64, 1)
        two = jnp.where(mid, w, v) + pltpu.roll(jnp.where(mid, v, w), 64, 1)
        put(j, jnp.where(even, one, two) + pltpu.roll(jnp.where(even, two, one), 96, 1))
        return carry

    lax.fori_loop(0, packs, segments, 0)
    aim = summed(rank)
    aim = aim + pltpu.roll(aim, 64, 1)
    put(packs, aim + pltpu.roll(aim, 32, 1))

    pay_copies = []
    for d in range(1, n_item):
        to = lax.rem(me_i + d, n_item)
        copy = pltpu.make_async_remote_copy(
            src_ref=pay.at[to], dst_ref=recv.at[d], send_sem=pay_send.at[d], recv_sem=pay_recv.at[d],
            device_id={"item": to}, device_id_type=MESH,
        )
        copy.start()
        pay_copies.append(copy)
    for copy in pay_copies:
        copy.wait()
    total = pay[me_i]
    for d in range(1, n_item):
        total = total + recv[d]
    answer = solve([total[j] for j in range(packs)], total[packs])

    xg[me_i] = answer
    x_copies = []
    for d in range(1, n_item):
        copy = pltpu.make_async_remote_copy(
            src_ref=xg.at[me_i], dst_ref=xg.at[me_i], send_sem=x_send.at[d], recv_sem=x_recv.at[d],
            device_id={"item": lax.rem(me_i + d, n_item)}, device_id_type=MESH,
        )
        copy.start()
        x_copies.append(copy)
    for d in range(1, n_item):
        x_copies[d - 1].wait_send()
        source = lax.rem(me_i + n_item - d, n_item)
        pltpu.make_async_remote_copy(
            src_ref=xg.at[source], dst_ref=xg.at[source], send_sem=x_send.at[d], recv_sem=x_recv.at[d],
            device_id={"item": lax.rem(me_i + d, n_item)}, device_id_type=MESH,
        ).wait_recv()
    for q in range(n_item):
        out[q * per : (q + 1) * per, :] = xg[q, 0:per, 0:rank]


def solution(mesh):
    n_user, n_item = mesh.shape["user"], mesh.shape["item"]
    placed = (
        P("user", "item", None, None),
        P("user", "item", None),
        P("user", "item", None),
        P("user", "item", None),
        P("user", "item"),
        P(),
        P(("item", "user"), None),
        P(),
    )

    def local(values, block_user, block_item, block_ctx, block_count, core, item_factor, ctx_factor):
        rank = core.shape[0]
        slots, bw = values.shape[2], values.shape[3]
        quarter = item_factor.shape[0] // 4
        packs = rank // 4
        return pl.pallas_call(
            functools.partial(kernel, n_user, n_item),
            out_shape=jax.ShapeDtypeStruct((U_SH, rank), F32),
            in_specs=[pl.BlockSpec(memory_space=pltpu.VMEM)] * 8,
            out_specs=pl.BlockSpec(memory_space=pltpu.VMEM),
            scratch_shapes=[
                pltpu.VMEM((n_user, quarter, 128), BF16),
                pltpu.VMEM((slots, 128), jnp.int32),
                pltpu.VMEM((4, ctx_factor.shape[0], 128), BF16),
                pltpu.VMEM((packs, slots, 128), BF16),
                pltpu.VMEM(((rank + 2) * slots, bw), F32),
                pltpu.VMEM(((rank + 1) * slots, 128), F32),
                pltpu.VMEM((n_item, packs + 1, 8, 128), F32),
                pltpu.VMEM((n_item, packs + 1, 8, 128), F32),
                pltpu.VMEM((n_item, 8, 128), F32),
                pltpu.SemaphoreType.DMA((n_user,)),
                pltpu.SemaphoreType.DMA((n_user,)),
                pltpu.SemaphoreType.DMA((n_item,)),
                pltpu.SemaphoreType.DMA((n_item,)),
                pltpu.SemaphoreType.DMA((n_item,)),
                pltpu.SemaphoreType.DMA((n_item,)),
            ],
            compiler_params=pltpu.CompilerParams(
                collective_id=0, has_side_effects=True, vmem_limit_bytes=40 * 1024 * 1024
            ),
        )(values, block_user, block_item, block_ctx, block_count, core, item_factor, ctx_factor)

    return jax.shard_map(local, mesh=mesh, in_specs=placed, out_specs=P("user", None), check_vma=False)
```

profile of v0, /device:TPU:0, one launch (start us, length us, event | category | flops | bytes accessed | tf_op | source)
XLA Modules:
  0.0 38.1 jit_solution(5562016140797283153)
XLA Ops:
  0.7 0.0 copy-start.5
  0.7 0.8 %copy.10.ctx = bf16[256,32]{1,0:T(8,128)(2,1)S(1)} copy(bf16[256,32]{0,1:T(8,128)(2,1)} %param.15) | data formatting | bytes 32768 | tf_op args[7]
  1.5 0.0 copy-done.5
  1.5 0.0 copy-start.1
  1.5 0.0 copy-start.2
  1.5 0.0 copy-start.3
  1.5 0.0 copy-start.4
  1.6 0.1 copy.9.item
  1.7 0.7 %copy-done.1 = bf16[1,1,256,128]{3,2,1,0:T(8,128)(2,1)S(1)} copy-done((bf16[1,1,256,128]{3,2,1,0:T(8,128)(2,1)S(1)}, bf16[1,1,256,128]{3,2,1,0:T(8,128)(2,1)}, u32[]{:S(2)}) %copy-start.1) | copy-done | bytes 65560
  2.4 0.0 copy-done.2
  2.4 0.0 copy-done.3
  2.4 0.0 copy-done.4
  2.4 0.0 copy-start
  2.4 0.9 %copy-done = bf16[32,32,32]{2,1,0:T(8,128)(2,1)S(1)} copy-done((bf16[32,32,32]{2,1,0:T(8,128)(2,1)S(1)}, bf16[32,32,32]{2,1,0:T(8,128)(2,1)}, u32[]{:S(2)}) %copy-start) | copy-done | bytes 65560
  3.3 34.1 %shard_map.82 = f32[64,32]{1,0:T(8,128)S(1)} custom-call(bf16[1,1,256,128]{3,2,1,0:T(8,128)(2,1)S(1)} %copy-done.1, s32[1,1,256]{2,1,0:T(1,128)S(1)} %copy-done.2, s32[1,1,256]{2,1,0:T(1,128)S(1)} %copy-done.3, s32[1,1,256]{2,1,0:T(1,128)S(1)} %copy-done.4, s32[1,1]{1,0:T(1,128)S(6)} %copy.12.b_count, bf16[32,32,32]{2,1,0:T(8,128)(2,1)S(1)} %copy-done, ...), custom_call_target="tpu_custom_call" | custom-call | tf_op jit(solution)/shard_map/pallas_call | solution.py:233
  37.4 0.7 %copy.11 = f32[64,32]{0,1:T(8,128)} copy(f32[64,32]{1,0:T(8,128)S(1)} %shard_map.82) | data formatting | bytes 16384 | tf_op jit(solution)/shard_map/pallas_call | solution.py:233
Async XLA Ops:
  0.7 0.9 %copy-start.5 = (bf16[512,32]{0,1:T(8,128)(2,1)S(1)}, bf16[512,32]{0,1:T(8,128)(2,1)}, u32[]{:S(2)}) copy-start(bf16[512,32]{0,1:T(8,128)(2,1)} %param.14) | copy-start | bytes 98308
  1.5 0.8 %copy-start.1 = (bf16[1,1,256,128]{3,2,1,0:T(8,128)(2,1)S(1)}, bf16[1,1,256,128]{3,2,1,0:T(8,128)(2,1)}, u32[]{:S(2)}) copy-start(bf16[1,1,256,128]{3,2,1,0:T(8,128)(2,1)} %values.1) | copy-start | bytes 196612
  1.5 0.8 %copy-start.2 = (s32[1,1,256]{2,1,0:T(1,128)S(1)}, s32[1,1,256]{2,1,0:T(1,128)}, u32[]{:S(2)}) copy-start(s32[1,1,256]{2,1,0:T(1,128)} %b_user.1) | copy-start | bytes 3076
  1.5 0.8 %copy-start.3 = (s32[1,1,256]{2,1,0:T(1,128)S(1)}, s32[1,1,256]{2,1,0:T(1,128)}, u32[]{:S(2)}) copy-start(s32[1,1,256]{2,1,0:T(1,128)} %b_item.1) | copy-start | bytes 3076
  1.5 0.8 %copy-start.4 = (s32[1,1,256]{2,1,0:T(1,128)S(1)}, s32[1,1,256]{2,1,0:T(1,128)}, u32[]{:S(2)}) copy-start(s32[1,1,256]{2,1,0:T(1,128)} %b_ctx.1) | copy-start | bytes 3076
  2.4 1.0 %copy-start = (bf16[32,32,32]{2,1,0:T(8,128)(2,1)S(1)}, bf16[32,32,32]{2,1,0:T(8,128)(2,1)}, u32[]{:S(2)}) copy-start(bf16[32,32,32]{2,1,0:T(8,128)(2,1)} %core.1) | copy-start | bytes 196612
where the time goes:
time: 38.4 us; the launch traced here: 38.1 us
  Pallas kernels  34.1 us (89%)
  local copies, waits for them, and re-layouts  3.29 us (9%)
  between operations  0.72 us (2%)
    pallas_call x1, Pallas kernels, local(): pl.pallas_call(functools.partial(kernel, n_user, n_item), out_shape=jax.S...  34.1 us
    unnamed x14, local copies, waits for them, and re-layouts  2.61 us

commit v1 on v0

v1 whole, which is shorter than its diff:
```python
import functools

import jax
import jax.numpy as jnp
from jax import lax
from jax.experimental import pallas as pl
from jax.experimental.pallas import tpu as pltpu
from jax.sharding import PartitionSpec as P

U_SH = 64
RIDGE = 0.1
MESH = pl.DeviceIdType.MESH
F32 = jnp.float32
BF16 = jnp.bfloat16
NT = (((1,), (1,)), ((), ()))


def iota(shape, dim):
    return lax.broadcasted_iota(jnp.int32, shape, dim)


def lanes_of(x, index):
    return jnp.take_along_axis(x, index, axis=1, mode="promise_in_bounds")


def solve(mats, target):
    shape = mats[0].shape
    lane = iota(shape, 1)
    block, place = lane >> 5, lane & 31
    count = len(mats)
    mats = [m + jnp.where(place == 4 * j + block, RIDGE, 0.0) for j, m in enumerate(mats)]
    cols = [lanes_of(target, 4 * j + block) for j in range(count)]
    own = [jnp.zeros(shape, F32)] * count
    off = [jnp.zeros(shape, F32)] * count
    for k in range(0, 4 * count, 2):
        jk, ck = divmod(k, 4)
        pair = mats[jk]
        p, s, q = (lanes_of(pair, jnp.full(shape, i, jnp.int32)) for i in (ck * 32 + k, ck * 32 + k + 1, ck * 32 + 33 + k))
        row0, row1 = (lanes_of(pair, (ck + i) * 32 + place) for i in (0, 1))
        rhs0, rhs1 = (lanes_of(cols[jk], (ck + i) * 32 + place) for i in (0, 1))
        factor0 = [lanes_of(m, (block << 5) + k) for m in mats]
        factor1 = [lanes_of(m, (block << 5) + k + 1) for m in mats]
        here = (block >> 1) == ck // 2
        factor0[jk], factor1[jk] = jnp.where(here, 0.0, factor0[jk]), jnp.where(here, 0.0, factor1[jk])
        inverse = 1.0 / (p * q - s * s)
        p, s, q = p * inverse, s * inverse, q * inverse
        own[jk] = jnp.where(here, jnp.where((block & 1) == 0, q, p), own[jk])
        off[jk] = jnp.where(here, s, off[jk])
        row0, row1 = q * row0 - s * row1, p * row1 - s * row0
        rhs0, rhs1 = q * rhs0 - s * rhs1, p * rhs1 - s * rhs0
        mats = [m - (f0 * row0 + f1 * row1) for m, f0, f1 in zip(mats, factor0, factor1)]
        cols = [c - (f0 * rhs0 + f1 * rhs1) for c, f0, f1 in zip(cols, factor0, factor1)]
    answer = jnp.zeros(shape, F32)
    for j in range(count):
        x = own[j] * cols[j] - off[j] * lanes_of(cols[j], (block ^ 1) << 5)
        answer = jnp.where((lane >> 2) == j, lanes_of(x, (lane & 3) << 5), answer)
    return answer


def kernel(
    n_user, n_item,
    values_hbm, user_hbm, item_hbm, ctx_hbm, count_hbm, core_hbm, rows_hbm, slab_hbm, out,
    values, b_user, b_item, b_ctx, b_count, core, slab,
    fac, starts, bt, yb, rf, gb, pay, recv, xg,
    load, fac_send, fac_recv, pay_send, pay_recv, x_send, x_recv,
):
    me_u, me_i = lax.axis_index("user"), lax.axis_index("item")
    slots, bw = values.shape
    rank = core.shape[0]
    rows = rows_hbm.shape[1]
    packs = rank // 4
    per = U_SH // n_item

    barrier = pltpu.get_barrier_semaphore()
    for d in range(1, n_user):
        pl.semaphore_signal(barrier, inc=1, device_id={"user": lax.rem(me_u + d, n_user)}, device_id_type=MESH)
    for d in range(1, n_item):
        pl.semaphore_signal(barrier, inc=1, device_id={"item": lax.rem(me_i + d, n_item)}, device_id_type=MESH)

    loads = [
        pltpu.make_async_copy(source, target, load.at[i])
        for i, (source, target) in enumerate((
            (ctx_hbm.at[0], b_ctx), (item_hbm.at[0], b_item), (user_hbm.at[0], b_user), (count_hbm, b_count),
            (values_hbm.at[0, 0], values), (rows_hbm, fac.at[0]), (core_hbm, core), (slab_hbm, slab),
        ))
    ]
    for copy in loads:
        copy.start()
    pl.semaphore_wait(barrier, n_user + n_item - 2)
    fac_copies = []
    for d in range(1, n_user):
        copy = pltpu.make_async_remote_copy(
            src_ref=rows_hbm, dst_ref=fac.at[d], send_sem=fac_send.at[d], recv_sem=fac_recv.at[d],
            device_id={"user": lax.rem(me_u + d, n_user)}, device_id_type=MESH,
        )
        copy.start()
        fac_copies.append(copy)
    for copy in loads:
        copy.wait()

    ids = b_item[...]
    parts = [jnp.broadcast_to(r.astype(F32), (128, slots)) for r in (b_ctx[...], ids >> 7, ids & 127)]
    eye = (iota((slots, slots), 0) == iota((slots, slots), 1)).astype(F32).astype(BF16)
    columns = lax.dot_general(eye, jnp.concatenate(parts, axis=0).astype(BF16), NT, preferred_element_type=F32)
    start_col = columns[:, :128].astype(jnp.int32)
    item_col = (columns[:, 128:256] * 128.0 + columns[:, 256:384]).astype(jnp.int32)
    starts[...] = start_col

    turned = values[...].astype(F32)
    for bit in range(bw.bit_length() - 1):
        turned = jnp.where(((start_col >> bit) & 1) == 1, pltpu.roll(turned, 1 << bit, 1), turned)
    rf[pl.ds(rank * slots, slots), :] = turned
    rf[pl.ds((rank + 1) * slots, slots), :] = jnp.zeros((slots, bw), F32)

    cores = core[...].astype(F32)
    mixing = jnp.concatenate([cores[a] for a in range(rank)], axis=1).astype(BF16)
    for c in range(4):
        pieces = [jnp.zeros(slab.shape, BF16)] * 4
        pieces[c] = slab[...]
        bt[c] = jnp.concatenate(pieces, axis=0)
    live = iota((U_SH, slots), 1) < b_count[...]
    onehot = jnp.where((iota((U_SH, slots), 0) == b_user[...]) & live, 1.0, 0.0).astype(BF16)

    wanted = jnp.concatenate([item_col] * (rows // 128), axis=1)
    lane = iota((slots, rows), 1)
    chosen = jnp.zeros((slots, rank), F32)
    for d in range(n_user):
        held = lax.rem(me_u + n_user - d, n_user) * rows
        picks = jnp.where(lane + held == wanted, 1.0, 0.0).astype(BF16)
        if d:
            fac_copies[d - 1].wait()
        chosen = chosen + lax.dot_general(picks, fac[d], NT, preferred_element_type=F32)
    proj = jnp.dot(chosen.astype(BF16), mixing, preferred_element_type=F32).astype(BF16)
    for j in range(packs):
        yb[j] = proj[:, 128 * j : 128 * (j + 1)]

    def features(j, carry):
        first = iota((slots, bw), 1) >= starts[...]
        z = yb[j]
        for c in range(4):
            full = jnp.dot(z, bt[c], preferred_element_type=F32)
            rf[pl.ds(pl.multiple_of((4 * j + c) * slots, slots), slots), :] = jnp.where(first, full[:, :bw], full[:, bw:])
        return carry

    lax.fori_loop(0, packs, features, 0)

    unrolled = 4

    def grams(turn, carry):
        sub, ln = iota((8, 128), 0), iota((8, 128), 1)
        low, same = sub < 4, (ln >> 5) == (sub & 3)
        bases = [pl.multiple_of(8 * (unrolled * turn + i), 8) for i in range(unrolled)]
        kept = []
        for base in bases:
            left = jnp.concatenate([rf[pl.ds(a * slots + base, 8), :] for a in range(rank + 2)], axis=0).astype(BF16)
            right = jnp.concatenate([rf[pl.ds(base + s, rank, stride=slots), :] for s in range(8)], axis=0).astype(BF16)
            kept.append(lax.dot_general(left, right, NT, preferred_element_type=F32))
        for base, full in zip(bases, kept):
            for a in range(rank + 1):
                part = full[8 * a : 8 * a + 8]
                gb[pl.ds(a * slots + base, 8), :] = jnp.where(same, jnp.where(low, part[:, :128], part[:, 128:]), 0.0)
        return carry

    lax.fori_loop(0, slots // (8 * unrolled), grams, 0)

    def summed(a):
        x = gb[pl.ds(a * slots, slots), :]
        high = x.astype(BF16)
        rest = (x - high.astype(F32)).astype(BF16)
        both = jnp.dot(onehot, jnp.concatenate([high, rest], axis=1), preferred_element_type=F32)
        return both[:, :128] + both[:, 128:]

    if per < 8:
        pay[...] = jnp.zeros(pay.shape, F32)

    def put(j, x):
        for q in range(n_item):
            pay[q, j, 0:per, :] = x[q * per : (q + 1) * per]

    blk = iota((U_SH, 128), 1) >> 5
    low, mid, even = blk < 2, (blk == 1) | (blk == 2), (blk & 1) == 0
    pay_copies = []
    bounds = [0, 3, 6, packs + 1]
    for part, (begin, end) in enumerate(zip(bounds[:-1], bounds[1:])):
        for j in range(begin, end):
            if j < packs:
                x, w, y, v = (summed(4 * j + c) for c in range(4))
                one = jnp.where(low, x, y) + pltpu.roll(jnp.where(low, y, x), 64, 1)
                two = jnp.where(mid, w, v) + pltpu.roll(jnp.where(mid, v, w), 64, 1)
                put(j, jnp.where(even, one, two) + pltpu.roll(jnp.where(even, two, one), 96, 1))
            else:
                aim = summed(rank)
                aim = aim + pltpu.roll(aim, 64, 1)
                put(j, aim + pltpu.roll(aim, 32, 1))
        for d in range(1, n_item):
            to = lax.rem(me_i + d, n_item)
            copy = pltpu.make_async_remote_copy(
                src_ref=pay.at[to, begin:end], dst_ref=recv.at[d, begin:end],
                send_sem=pay_send.at[part, d], recv_sem=pay_recv.at[part, d],
                device_id={"item": to}, device_id_type=MESH,
            )
            copy.start()
            pay_copies.append(copy)
    for copy in pay_copies:
        copy.wait()
    total = pay[me_i]
    for d in range(1, n_item):
        total = total + recv[d]
    answer = solve([total[j] for j in range(packs)], total[packs])

    xg[me_i] = answer
    x_copies = []
    for d in range(1, n_item):
        copy = pltpu.make_async_remote_copy(
            src_ref=xg.at[me_i], dst_ref=xg.at[me_i], send_sem=x_send.at[d], recv_sem=x_recv.at[d],
            device_id={"item": lax.rem(me_i + d, n_item)}, device_id_type=MESH,
        )
        copy.start()
        x_copies.append(copy)
    for d in range(1, n_item):
        x_copies[d - 1].wait_send()
        source = lax.rem(me_i + n_item - d, n_item)
        pltpu.make_async_remote_copy(
            src_ref=xg.at[source], dst_ref=xg.at[source], send_sem=x_send.at[d], recv_sem=x_recv.at[d],
            device_id={"item": lax.rem(me_i + d, n_item)}, device_id_type=MESH,
        ).wait_recv()
    for q in range(n_item):
        out[q * per : (q + 1) * per, :] = xg[q, 0:per, 0:rank]


def solution(mesh):
    n_user, n_item = mesh.shape["user"], mesh.shape["item"]
    placed = (
        P("user", "item", None, None),
        P("user", "item", None),
        P("user", "item", None),
        P("user", "item", None),
        P("user", "item"),
        P(),
        P(("item", "user"), None),
        P(),
    )

    def local(values, block_user, block_item, block_ctx, block_count, core, item_factor, ctx_factor):
        rank = core.shape[0]
        slots, bw = values.shape[2], values.shape[3]
        packs = rank // 4
        return pl.pallas_call(
            functools.partial(kernel, n_user, n_item),
            out_shape=jax.ShapeDtypeStruct((U_SH, rank), F32),
            in_specs=[pl.BlockSpec(memory_space=pltpu.HBM)] * 8,
            out_specs=pl.BlockSpec(memory_space=pltpu.VMEM),
            scratch_shapes=[
                pltpu.VMEM((slots, bw), BF16),
                pltpu.VMEM((1, slots), jnp.int32),
                pltpu.VMEM((1, slots), jnp.int32),
                pltpu.VMEM((1, slots), jnp.int32),
                pltpu.VMEM((1, 1), jnp.int32),
                pltpu.VMEM(core.shape, BF16),
                pltpu.VMEM((rank, ctx_factor.shape[0]), BF16),
                pltpu.VMEM((n_user, rank, item_factor.shape[0]), BF16),
                pltpu.VMEM((slots, 128), jnp.int32),
                pltpu.VMEM((4, 128, ctx_factor.shape[0]), BF16),
                pltpu.VMEM((packs, slots, 128), BF16),
                pltpu.VMEM(((rank + 2) * slots, bw), F32),
                pltpu.VMEM(((rank + 1) * slots, 128), F32),
                pltpu.VMEM((n_item, packs + 1, 8, 128), F32),
                pltpu.VMEM((n_item, packs + 1, 8, 128), F32),
                pltpu.VMEM((n_item, 8, 128), F32),
                pltpu.SemaphoreType.DMA((8,)),
                pltpu.SemaphoreType.DMA((n_user,)),
                pltpu.SemaphoreType.DMA((n_user,)),
                pltpu.SemaphoreType.DMA((3, n_item)),
                pltpu.SemaphoreType.DMA((3, n_item)),
                pltpu.SemaphoreType.DMA((n_item,)),
                pltpu.SemaphoreType.DMA((n_item,)),
            ],
            compiler_params=pltpu.CompilerParams(
                collective_id=0, has_side_effects=True, vmem_limit_bytes=60 * 1024 * 1024
            ),
        )(
            values, block_user, block_item, block_ctx, block_count, core,
            jnp.transpose(item_factor), jnp.transpose(ctx_factor),
        )

    return jax.shard_map(local, mesh=mesh, in_specs=placed, out_specs=P("user", None), check_vma=False)
```

time: 38.4 us -> 30.6 us (0.80)
  Pallas kernels: 34.1 us -> 28.3 us
  local copies, waits for them, and re-layouts: 3.29 us -> 1.44 us
    pallas_call x1, Pallas kernels: 34.1 us -> 28.3 us  [local(): pl.pallas_call(functools.partial(kernel, n_user, n_item), out_shape=jax.S...]
    unnamed x14 -> x0, local copies, waits for them, and re-layouts: 2.61 us -> none
    pallas_call x1, local copies, waits for them, and re-layouts: 0.68 us -> 1.44 us  [local(): pl.pallas_call(functools.partial(kernel, n_user, n_item), out_shape=jax.S...]
where the time goes in v1:
time: 30.6 us; the launch traced here: 30.4 us
  Pallas kernels  28.3 us (92%)
  local copies, waits for them, and re-layouts  1.44 us (5%)
  between operations  0.66 us (2%)
    pallas_call x1, Pallas kernels, local(): pl.pallas_call(functools.partial(kernel, n_user, n_item), out_shape=jax.S...  28.3 us
    pallas_call x1, local copies, waits for them, and re-layouts, local(): pl.pallas_call(functools.partial(kernel, n_user, n_item), out_shape=jax.S...  1.44 us

profile of v1, /device:TPU:0, one launch (start us, length us, event | category | flops | bytes accessed | tf_op | source)
XLA Modules:
  0.0 30.4 jit_solution(152681394720982112)
XLA Ops:
  0.7 28.3 %shard_map.82 = f32[64,32]{1,0:T(8,128)} custom-call(bf16[1,1,256,128]{3,2,1,0:T(8,128)(2,1)} %values_hbm.1, s32[1,1,256]{2,1,0:T(1,128)} %user_hbm.1, s32[1,1,256]{2,1,0:T(1,128)} %item_hbm.1, s32[1,1,256]{2,1,0:T(1,128)} %ctx_hbm.1, s32[1,1]{1,0:T(1,128)S(6)} %copy.10.count_hbm, bf16[32,32,32]{2,1,0:T(8,128)(2,1)} %core_hbm.1, bf16[32,512]{1,0:T(8,128)(2,1)} %bitcast.2, ...), custom_call_target="tpu_custom_call" | custom-call | tf_op jit(solution)/shard_map/pallas_call | solution.py:248
  28.9 1.4 %copy.9 = f32[64,32]{0,1:T(8,128)} copy(f32[64,32]{1,0:T(8,128)} %shard_map.82) | data formatting | bytes 16384 | tf_op jit(solution)/shard_map/pallas_call | solution.py:248

commit v2 on v1

--- a/solution.py
+++ b/solution.py
@@ -70,6 +70,7 @@
     rows = rows_hbm.shape[1]
     packs = rank // 4
     per = U_SH // n_item
+    pitch = slots + 8
 
     barrier = pltpu.get_barrier_semaphore()
     for d in range(1, n_user):
@@ -109,8 +110,8 @@
     turned = values[...].astype(F32)
     for bit in range(bw.bit_length() - 1):
         turned = jnp.where(((start_col >> bit) & 1) == 1, pltpu.roll(turned, 1 << bit, 1), turned)
-    rf[pl.ds(rank * slots, slots), :] = turned
-    rf[pl.ds((rank + 1) * slots, slots), :] = jnp.zeros((slots, bw), F32)
+    rf[pl.ds(rank * pitch, slots), :] = turned
+    rf[pl.ds((rank + 1) * pitch, slots), :] = jnp.zeros((slots, bw), F32)
 
     cores = core[...].astype(F32)
     mixing = jnp.concatenate([cores[a] for a in range(rank)], axis=1).astype(BF16)
@@ -134,17 +135,17 @@
     for j in range(packs):
         yb[j] = proj[:, 128 * j : 128 * (j + 1)]
 
-    def features(j, carry):
+    def features(turn, carry):
         first = iota((slots, bw), 1) >= starts[...]
-        z = yb[j]
-        for c in range(4):
-            full = jnp.dot(z, bt[c], preferred_element_type=F32)
-            rf[pl.ds(pl.multiple_of((4 * j + c) * slots, slots), slots), :] = jnp.where(first, full[:, :bw], full[:, bw:])
+        for i in range(8):
+            j, c = 2 * turn + i // 4, i % 4
+            full = jnp.dot(yb[j], bt[c], preferred_element_type=F32)
+            rf[pl.ds(pl.multiple_of((4 * j + c) * pitch, 8), slots), :] = jnp.where(first, full[:, :bw], full[:, bw:])
         return carry
 
-    lax.fori_loop(0, packs, features, 0)
-
-    unrolled = 4
+    lax.fori_loop(0, packs // 2, features, 0)
+
+    unrolled = 8
 
     def grams(turn, carry):
         sub, ln = iota((8, 128), 0), iota((8, 128), 1)
@@ -152,8 +153,8 @@
         bases = [pl.multiple_of(8 * (unrolled * turn + i), 8) for i in range(unrolled)]
         kept = []
         for base in bases:
-            left = jnp.concatenate([rf[pl.ds(a * slots + base, 8), :] for a in range(rank + 2)], axis=0).astype(BF16)
-            right = jnp.concatenate([rf[pl.ds(base + s, rank, stride=slots), :] for s in range(8)], axis=0).astype(BF16)
+            left = jnp.concatenate([rf[pl.ds(a * pitch + base, 8), :] for a in range(rank + 2)], axis=0).astype(BF16)
+            right = jnp.concatenate([rf[pl.ds(base + s, rank, stride=pitch), :] for s in range(8)], axis=0).astype(BF16)
             kept.append(lax.dot_general(left, right, NT, preferred_element_type=F32))
         for base, full in zip(bases, kept):
             for a in range(rank + 1):
@@ -180,11 +181,11 @@
     blk = iota((U_SH, 128), 1) >> 5
     low, mid, even = blk < 2, (blk == 1) | (blk == 2), (blk & 1) == 0
     pay_copies = []
-    bounds = [0, 3, 6, packs + 1]
+    bounds = [0, 4, 7, packs + 1]
     for part, (begin, end) in enumerate(zip(bounds[:-1], bounds[1:])):
         for j in range(begin, end):
-            if j < packs:
-                x, w, y, v = (summed(4 * j + c) for c in range(4))
+            if j:
+                x, w, y, v = (summed(4 * j - 4 + c) for c in range(4))
                 one = jnp.where(low, x, y) + pltpu.roll(jnp.where(low, y, x), 64, 1)
                 two = jnp.where(mid, w, v) + pltpu.roll(jnp.where(mid, v, w), 64, 1)
                 put(j, jnp.where(even, one, two) + pltpu.roll(jnp.where(even, two, one), 96, 1))
@@ -206,7 +207,7 @@
     total = pay[me_i]
     for d in range(1, n_item):
         total = total + recv[d]
-    answer = solve([total[j] for j in range(packs)], total[packs])
+    answer = solve([total[j + 1] for j in range(packs)], total[0])
 
     xg[me_i] = answer
     x_copies = []
@@ -224,8 +225,8 @@
             src_ref=xg.at[source], dst_ref=xg.at[source], send_sem=x_send.at[d], recv_sem=x_recv.at[d],
             device_id={"item": lax.rem(me_i + d, n_item)}, device_id_type=MESH,
         ).wait_recv()
-    for q in range(n_item):
-        out[q * per : (q + 1) * per, :] = xg[q, 0:per, 0:rank]
+    solved = jnp.concatenate([xg[q, 0:per, :] for q in range(n_item)] + [jnp.zeros((128 - U_SH, 128), F32)], axis=0)
+    out[...] = jnp.transpose(solved)[:rank, :U_SH]
 
 
 def solution(mesh):
@@ -245,9 +246,9 @@
         rank = core.shape[0]
         slots, bw = values.shape[2], values.shape[3]
         packs = rank // 4
-        return pl.pallas_call(
+        solved = pl.pallas_call(
             functools.partial(kernel, n_user, n_item),
-            out_shape=jax.ShapeDtypeStruct((U_SH, rank), F32),
+            out_shape=jax.ShapeDtypeStruct((rank, U_SH), F32),
             in_specs=[pl.BlockSpec(memory_space=pltpu.HBM)] * 8,
             out_specs=pl.BlockSpec(memory_space=pltpu.VMEM),
             scratch_shapes=[
@@ -262,7 +263,7 @@
                 pltpu.VMEM((slots, 128), jnp.int32),
                 pltpu.VMEM((4, 128, ctx_factor.shape[0]), BF16),
                 pltpu.VMEM((packs, slots, 128), BF16),
-                pltpu.VMEM(((rank + 2) * slots, bw), F32),
+                pltpu.VMEM(((rank + 2) * (slots + 8), bw), F32),
                 pltpu.VMEM(((rank + 1) * slots, 128), F32),
                 pltpu.VMEM((n_item, packs + 1, 8, 128), F32),
                 pltpu.VMEM((n_item, packs + 1, 8, 128), F32),
@@ -282,5 +283,6 @@
             values, block_user, block_item, block_ctx, block_count, core,
             jnp.transpose(item_factor), jnp.transpose(ctx_factor),
         )
+        return jnp.transpose(solved)
 
     return jax.shard_map(local, mesh=mesh, in_specs=placed, out_specs=P("user", None), check_vma=False)

time: 30.6 us -> 28 us (0.915)
  Pallas kernels: 28.3 us -> 25.8 us
    pallas_call x1, Pallas kernels: 28.3 us -> 25.8 us  [local(): pl.pallas_call(functools.partial(kernel, n_user, n_item), out_shape=jax.S...]
    pallas_call x1 -> x0, local copies, waits for them, and re-layouts: 1.44 us -> none  [local(): pl.pallas_call(functools.partial(kernel, n_user, n_item), out_shape=jax.S...]
    unnamed x0 -> x1, local copies, waits for them, and re-layouts: none -> 1.32 us
where the time goes in v2:
time: 28 us; the launch traced here: 27.8 us
  Pallas kernels  25.8 us (92%)
  local copies, waits for them, and re-layouts  1.32 us (5%)
  between operations  0.66 us (2%)
    pallas_call x1, Pallas kernels, local(): pl.pallas_call(functools.partial(kernel, n_user, n_item), out_shape=jax.S...  25.8 us
    unnamed x1, local copies, waits for them, and re-layouts  1.32 us

profile of v2, /device:TPU:0, one launch (start us, length us, event | category | flops | bytes accessed | tf_op | source)
XLA Modules:
  0.0 27.8 jit_solution(15109245658330296955)
XLA Ops:
  0.7 25.8 %shard_map.82 = f32[32,64]{1,0:T(8,128)} custom-call(bf16[1,1,256,128]{3,2,1,0:T(8,128)(2,1)} %values_hbm.1, s32[1,1,256]{2,1,0:T(1,128)} %user_hbm.1, s32[1,1,256]{2,1,0:T(1,128)} %item_hbm.1, s32[1,1,256]{2,1,0:T(1,128)} %ctx_hbm.1, s32[1,1]{1,0:T(1,128)S(6)} %copy.10.count_hbm, bf16[32,32,32]{2,1,0:T(8,128)(2,1)} %core_hbm.1, bf16[32,512]{1,0:T(8,128)(2,1)} %bitcast.4, ...), custom_call_target="tpu_custom_call" | custom-call | tf_op jit(solution)/shard_map/pallas_call | solution.py:249
  26.4 1.3 %copy.11 = f32[64,32]{0,1:T(8,128)} copy(f32[64,32]{0,1:T(8,128)} %bitcast.3) | data formatting | bytes 16384

commit v3 on v2

--- a/solution.py
+++ b/solution.py
@@ -145,30 +145,31 @@
 
     lax.fori_loop(0, packs // 2, features, 0)
 
-    unrolled = 8
+    turns = 2
 
     def grams(turn, carry):
         sub, ln = iota((8, 128), 0), iota((8, 128), 1)
         low, same = sub < 4, (ln >> 5) == (sub & 3)
-        bases = [pl.multiple_of(8 * (unrolled * turn + i), 8) for i in range(unrolled)]
-        kept = []
-        for base in bases:
-            left = jnp.concatenate([rf[pl.ds(a * pitch + base, 8), :] for a in range(rank + 2)], axis=0).astype(BF16)
-            right = jnp.concatenate([rf[pl.ds(base + s, rank, stride=pitch), :] for s in range(8)], axis=0).astype(BF16)
-            kept.append(lax.dot_general(left, right, NT, preferred_element_type=F32))
-        for base, full in zip(bases, kept):
+        for i in range(turns):
+            base = pl.multiple_of(16 * (turns * turn + i), 16)
+            kept = []
+            for begin in (base, base + 8):
+                left = jnp.concatenate([rf[pl.ds(a * pitch + begin, 8), :] for a in range(rank + 2)], axis=0).astype(BF16)
+                right = jnp.concatenate([rf[pl.ds(begin + s, rank, stride=pitch), :] for s in range(8)], axis=0).astype(BF16)
+                kept.append(lax.dot_general(left, right, NT, preferred_element_type=F32))
             for a in range(rank + 1):
-                part = full[8 * a : 8 * a + 8]
-                gb[pl.ds(a * slots + base, 8), :] = jnp.where(same, jnp.where(low, part[:, :128], part[:, 128:]), 0.0)
+                parts = [full[8 * a : 8 * a + 8] for full in kept]
+                parts = [jnp.where(same, jnp.where(low, p[:, :128], p[:, 128:]), 0.0) for p in parts]
+                part = jnp.concatenate(parts, axis=0)
+                high = part.astype(BF16)
+                gb[a, pl.ds(base, 16), 0:128] = high
+                gb[a, pl.ds(base, 16), 128:256] = (part - high.astype(F32)).astype(BF16)
         return carry
 
-    lax.fori_loop(0, slots // (8 * unrolled), grams, 0)
+    lax.fori_loop(0, slots // (16 * turns), grams, 0)
 
     def summed(a):
-        x = gb[pl.ds(a * slots, slots), :]
-        high = x.astype(BF16)
-        rest = (x - high.astype(F32)).astype(BF16)
-        both = jnp.dot(onehot, jnp.concatenate([high, rest], axis=1), preferred_element_type=F32)
+        both = jnp.dot(onehot, gb[a], preferred_element_type=F32)
         return both[:, :128] + both[:, 128:]
 
     if per < 8:
@@ -264,7 +265,7 @@
                 pltpu.VMEM((4, 128, ctx_factor.shape[0]), BF16),
                 pltpu.VMEM((packs, slots, 128), BF16),
                 pltpu.VMEM(((rank + 2) * (slots + 8), bw), F32),
-                pltpu.VMEM(((rank + 1) * slots, 128), F32),
+                pltpu.VMEM((rank + 1, slots, 256), BF16),
                 pltpu.VMEM((n_item, packs + 1, 8, 128), F32),
                 pltpu.VMEM((n_item, packs + 1, 8, 128), F32),
                 pltpu.VMEM((n_item, 8, 128), F32),

time: 28 us -> 28.7 us (1.025)
  Pallas kernels: 25.8 us -> 26.4 us
    pallas_call x1, Pallas kernels: 25.8 us -> 26.4 us  [local(): pl.pallas_call(functools.partial(kernel, n_user, n_item), out_shape=jax.S...]
where the time goes in v3:
time: 28.7 us; the launch traced here: 28.4 us
  Pallas kernels  26.4 us (92%)
  local copies, waits for them, and re-layouts  1.32 us (5%)
  between operations  0.66 us (2%)
    pallas_call x1, Pallas kernels, local(): pl.pallas_call(functools.partial(kernel, n_user, n_item), out_shape=jax.S...  26.4 us
    unnamed x1, local copies, waits for them, and re-layouts  1.32 us

profile of v3, /device:TPU:0, one launch (start us, length us, event | category | flops | bytes accessed | tf_op | source)
XLA Modules:
  0.0 28.4 jit_solution(17200471136239295518)
XLA Ops:
  0.7 26.4 %shard_map.82 = f32[32,64]{1,0:T(8,128)} custom-call(bf16[1,1,256,128]{3,2,1,0:T(8,128)(2,1)} %values_hbm.1, s32[1,1,256]{2,1,0:T(1,128)} %user_hbm.1, s32[1,1,256]{2,1,0:T(1,128)} %item_hbm.1, s32[1,1,256]{2,1,0:T(1,128)} %ctx_hbm.1, s32[1,1]{1,0:T(1,128)S(6)} %copy.10.count_hbm, bf16[32,32,32]{2,1,0:T(8,128)(2,1)} %core_hbm.1, bf16[32,512]{1,0:T(8,128)(2,1)} %bitcast.4, ...), custom_call_target="tpu_custom_call" | custom-call | tf_op jit(solution)/shard_map/pallas_call | solution.py:250
  27.1 1.3 %copy.11 = f32[64,32]{0,1:T(8,128)} copy(f32[64,32]{0,1:T(8,128)} %bitcast.3) | data formatting | bytes 16384

commit v4 on v2

--- a/solution.py
+++ b/solution.py
@@ -21,6 +21,10 @@
 
 def lanes_of(x, index):
     return jnp.take_along_axis(x, index, axis=1, mode="promise_in_bounds")
+
+
+def in_hbm(x):
+    return pltpu.with_memory_space_constraint(x, pltpu.HBM)
 
 
 def solve(mats, target):
@@ -137,32 +141,30 @@
 
     def features(turn, carry):
         first = iota((slots, bw), 1) >= starts[...]
-        for i in range(8):
-            j, c = 2 * turn + i // 4, i % 4
+        for i in range(rank):
+            j, c = i // 4, i % 4
             full = jnp.dot(yb[j], bt[c], preferred_element_type=F32)
-            rf[pl.ds(pl.multiple_of((4 * j + c) * pitch, 8), slots), :] = jnp.where(first, full[:, :bw], full[:, bw:])
+            rf[pl.ds((4 * j + c) * pitch, slots), :] = jnp.where(first, full[:, :bw], full[:, bw:])
         return carry
 
-    lax.fori_loop(0, packs // 2, features, 0)
-
-    unrolled = 8
+    features(0, 0)
+
+    unrolled = slots // 8
 
     def grams(turn, carry):
         sub, ln = iota((8, 128), 0), iota((8, 128), 1)
         low, same = sub < 4, (ln >> 5) == (sub & 3)
-        bases = [pl.multiple_of(8 * (unrolled * turn + i), 8) for i in range(unrolled)]
-        kept = []
+        bases = [8 * i for i in range(unrolled)]
         for base in bases:
             left = jnp.concatenate([rf[pl.ds(a * pitch + base, 8), :] for a in range(rank + 2)], axis=0).astype(BF16)
             right = jnp.concatenate([rf[pl.ds(base + s, rank, stride=pitch), :] for s in range(8)], axis=0).astype(BF16)
-            kept.append(lax.dot_general(left, right, NT, preferred_element_type=F32))
-        for base, full in zip(bases, kept):
+            full = lax.dot_general(left, right, NT, preferred_element_type=F32)
             for a in range(rank + 1):
                 part = full[8 * a : 8 * a + 8]
                 gb[pl.ds(a * slots + base, 8), :] = jnp.where(same, jnp.where(low, part[:, :128], part[:, 128:]), 0.0)
         return carry
 
-    lax.fori_loop(0, slots // (8 * unrolled), grams, 0)
+    grams(0, 0)
 
     def summed(a):
         x = gb[pl.ds(a * slots, slots), :]
@@ -248,7 +250,7 @@
         packs = rank // 4
         solved = pl.pallas_call(
             functools.partial(kernel, n_user, n_item),
-            out_shape=jax.ShapeDtypeStruct((rank, U_SH), F32),
+            out_shape=pltpu.VMEM((rank, U_SH), F32),
             in_specs=[pl.BlockSpec(memory_space=pltpu.HBM)] * 8,
             out_specs=pl.BlockSpec(memory_space=pltpu.VMEM),
             scratch_shapes=[
@@ -277,11 +279,11 @@
                 pltpu.SemaphoreType.DMA((n_item,)),
             ],
             compiler_params=pltpu.CompilerParams(
-                collective_id=0, has_side_effects=True, vmem_limit_bytes=60 * 1024 * 1024
+                collective_id=0, has_side_effects=True, vmem_limit_bytes=48 * 1024 * 1024
             ),
         )(
-            values, block_user, block_item, block_ctx, block_count, core,
-            jnp.transpose(item_factor), jnp.transpose(ctx_factor),
+            *(in_hbm(x) for x in (values, block_user, block_item, block_ctx)), block_count,
+            *(in_hbm(x) for x in (core, jnp.transpose(item_factor), jnp.transpose(ctx_factor))),
         )
         return jnp.transpose(solved)
 

time: 28 us -> 25.7 us (0.918)
  Pallas kernels: 25.8 us -> 24.2 us
  local copies, waits for them, and re-layouts: 1.32 us -> 0.61 us
    pallas_call x1, Pallas kernels: 25.8 us -> 24.2 us  [local(): pl.pallas_call(functools.partial(kernel, n_user, n_item), out_shape=pltpu...]
    unnamed x1, local copies, waits for them, and re-layouts: 1.32 us -> 0.61 us
where the time goes in v4:
time: 25.7 us; the launch traced here: 25.5 us
  Pallas kernels  24.2 us (94%)
  between operations  0.66 us (3%)
  local copies, waits for them, and re-layouts  0.61 us (2%)
    pallas_call x1, Pallas kernels, local(): pl.pallas_call(functools.partial(kernel, n_user, n_item), out_shape=pltpu...  24.2 us
    unnamed x1, local copies, waits for them, and re-layouts  0.61 us

profile of v4, /device:TPU:0, one launch (start us, length us, event | category | flops | bytes accessed | tf_op | source)
XLA Modules:
  0.0 25.5 jit_solution(2883211165494970676)
XLA Ops:
  0.7 24.2 %shard_map.82 = f32[32,64]{1,0:T(8,128)S(1)} custom-call(bf16[1,1,256,128]{3,2,1,0:T(8,128)(2,1)} %values_hbm.1, s32[1,1,256]{2,1,0:T(1,128)} %user_hbm.1, s32[1,1,256]{2,1,0:T(1,128)} %item_hbm.1, s32[1,1,256]{2,1,0:T(1,128)} %ctx_hbm.1, s32[1,1]{1,0:T(1,128)S(6)} %copy.11.count_hbm, bf16[32,32,32]{2,1,0:T(8,128)(2,1)} %core_hbm.1, ...), custom_call_target="tpu_custom_call" | custom-call | tf_op jit(solution)/shard_map/pallas_call | solution.py:251
  24.9 0.6 %copy.10 = f32[64,32]{0,1:T(8,128)} copy(f32[64,32]{0,1:T(8,128)S(1)} %bitcast.3) | data formatting | bytes 16384

commit v5 on v4

--- a/solution.py
+++ b/solution.py
@@ -139,32 +139,33 @@
     for j in range(packs):
         yb[j] = proj[:, 128 * j : 128 * (j + 1)]
 
-    def features(turn, carry):
-        first = iota((slots, bw), 1) >= starts[...]
-        for i in range(rank):
-            j, c = i // 4, i % 4
-            full = jnp.dot(yb[j], bt[c], preferred_element_type=F32)
-            rf[pl.ds((4 * j + c) * pitch, slots), :] = jnp.where(first, full[:, :bw], full[:, bw:])
-        return carry
-
-    features(0, 0)
-
-    unrolled = slots // 8
-
-    def grams(turn, carry):
-        sub, ln = iota((8, 128), 0), iota((8, 128), 1)
-        low, same = sub < 4, (ln >> 5) == (sub & 3)
-        bases = [8 * i for i in range(unrolled)]
-        for base in bases:
-            left = jnp.concatenate([rf[pl.ds(a * pitch + base, 8), :] for a in range(rank + 2)], axis=0).astype(BF16)
-            right = jnp.concatenate([rf[pl.ds(base + s, rank, stride=pitch), :] for s in range(8)], axis=0).astype(BF16)
-            full = lax.dot_general(left, right, NT, preferred_element_type=F32)
-            for a in range(rank + 1):
-                part = full[8 * a : 8 * a + 8]
-                gb[pl.ds(a * slots + base, 8), :] = jnp.where(same, jnp.where(low, part[:, :128], part[:, 128:]), 0.0)
-        return carry
-
-    grams(0, 0)
+    half = slots // 2
+    sub, ln = iota((8, 128), 0), iota((8, 128), 1)
+    upper, same = sub < 4, (ln >> 5) == (sub & 3)
+
+    def feature(begin, a):
+        first = iota((half, bw), 1) >= starts[pl.ds(begin, half), :]
+        full = jnp.dot(yb[a // 4, pl.ds(begin, half), :], bt[a % 4], preferred_element_type=F32)
+        rf[pl.ds(a * pitch + begin, half), :] = jnp.where(first, full[:, :bw], full[:, bw:])
+
+    def gram(base):
+        left = jnp.concatenate([rf[pl.ds(a * pitch + base, 8), :] for a in range(rank + 2)], axis=0).astype(BF16)
+        right = jnp.concatenate([rf[pl.ds(base + s, rank, stride=pitch), :] for s in range(8)], axis=0).astype(BF16)
+        full = lax.dot_general(left, right, NT, preferred_element_type=F32)
+        for a in range(rank + 1):
+            part = full[8 * a : 8 * a + 8]
+            gb[pl.ds(a * slots + base, 8), :] = jnp.where(same, jnp.where(upper, part[:, :128], part[:, 128:]), 0.0)
+
+    groups = half // 8
+    each = rank // groups
+    for a in range(rank):
+        feature(0, a)
+    for g in range(groups):
+        for a in range(each * g, each * (g + 1)):
+            feature(half, a)
+        gram(8 * g)
+    for g in range(groups):
+        gram(half + 8 * g)
 
     def summed(a):
         x = gb[pl.ds(a * slots, slots), :]

time: 25.7 us -> 25.8 us (level)
  no operation moved by 1% of the time
where the time goes in v5:
time: 25.8 us; the launch traced here: 25.6 us
  Pallas kernels  24.4 us (95%)
  between operations  0.66 us (3%)
  local copies, waits for them, and re-layouts  0.61 us (2%)
    pallas_call x1, Pallas kernels, local(): pl.pallas_call(functools.partial(kernel, n_user, n_item), out_shape=pltpu...  24.4 us
    unnamed x1, local copies, waits for them, and re-layouts  0.61 us

profile of v5, /device:TPU:0, one launch (start us, length us, event | category | flops | bytes accessed | tf_op | source)
XLA Modules:
  0.0 25.6 jit_solution(696384679320784637)
XLA Ops:
  0.7 24.4 %shard_map.82 = f32[32,64]{1,0:T(8,128)S(1)} custom-call(bf16[1,1,256,128]{3,2,1,0:T(8,128)(2,1)} %values_hbm.1, s32[1,1,256]{2,1,0:T(1,128)} %user_hbm.1, s32[1,1,256]{2,1,0:T(1,128)} %item_hbm.1, s32[1,1,256]{2,1,0:T(1,128)} %ctx_hbm.1, s32[1,1]{1,0:T(1,128)S(6)} %copy.11.count_hbm, bf16[32,32,32]{2,1,0:T(8,128)(2,1)} %core_hbm.1, ...), custom_call_target="tpu_custom_call" | custom-call | tf_op jit(solution)/shard_map/pallas_call | solution.py:252
  25.0 0.6 %copy.10 = f32[64,32]{0,1:T(8,128)} copy(f32[64,32]{0,1:T(8,128)S(1)} %bitcast.3) | data formatting | bytes 16384
